TPU v7x, 32 devices: a whole 2x2x4 slice. The times are simulated.
32 devices in a mesh: dp: 8 (over z, x), blk: 4 (over y, core).
Axes of the slice: x: 2, y: 2, z: 4, core: 2. Of those that a mesh axis runs over, the one named last changes fastest.
Arguments:
- block_input: bfloat16 [2, 32, 1024, 512], P(None, 'dp', 'blk'), may hold values from -6 to 6
- segment_ids: int32 [32, 1024], P('dp', 'blk'), may hold values from 0 to 3, as said below
- gain_one: float32 [512], replicated, may hold values from 0.5 to 1.5
- w_query: bfloat16 [512, 512], replicated, may hold values from -0.25 to 0.25
- w_key: bfloat16 [512, 512], replicated, may hold values from -0.25 to 0.25
- w_value: bfloat16 [512, 512], replicated, may hold values from -0.25 to 0.25
- w_out: bfloat16 [512, 512], replicated, may hold values from -1 to 1
- gain_two: float32 [512], replicated, may hold values from 0.5 to 1.5
- w_ctrl: bfloat16 [512, 2], replicated, may hold values from -0.1875 to 0.1875
- w_in: bfloat16 [2, 512, 2048], replicated, may hold values from -1.5 to 1.5
- w_back: bfloat16 [2, 2048, 512], replicated, may hold values from -3 to 3
- cotangent: bfloat16 [2, 32, 1024, 512], P(None, 'dp', 'blk'), may hold values from -6 to 6
Outputs:
- activations: bfloat16 [2, 32, 1024, 512], P(None, 'dp', 'blk')
- grad_input: bfloat16 [2, 32, 1024, 512], P(None, 'dp', 'blk')
- grad_gain_one: float32 [512], replicated
- grad_query: float32 [512, 512], replicated
- grad_key: float32 [512, 512], replicated
- grad_value: float32 [512, 512], replicated
- grad_out: float32 [512, 512], replicated
- grad_gain_two: float32 [512], replicated
- grad_ctrl: float32 [512, 2], replicated
- grad_in: float32 [2, 512, 2048], replicated
- grad_back: float32 [2, 2048, 512], replicated
Inputs may be any that keep to these rules, and one draw needn't show every extreme that they name: `segment_ids`: ids start at 0 and never fall along a row; they rise by one at each document start, and document k >= 1 begins fewer than 128 positions away from k * 256.
All inputs are finite; a program needn't handle non-finite values.
Results may differ from a plain program's by a relative error of at most 0.03.
Values may be sent and summed in bfloat16 or wider, within the bound.
A program may use at most 256 MiB of HBM per device.

v0:
```python
import functools

import jax
import jax.numpy as jnp
from jax import lax
from jax.experimental import pallas as pl
from jax.experimental.pallas import tpu as pltpu
from jax.sharding import PartitionSpec as P

HEAD_DIM = 64
GROUP = 32
EPSILON = 1e-05
BLOCK = 256
CHUNK = 512
SCALE = 0.125
MASKED = -1e30
VMEM_LIMIT = 60 * 1024 * 1024
BF = jnp.bfloat16
F32 = jnp.float32
MESH = pl.DeviceIdType.MESH


def dot(a, b, ca, cb):
    return lax.dot_general(a, b, (((ca,), (cb,)), ((), ())), preferred_element_type=F32)


def nn(a, b):
    return dot(a, b, 1, 0)


def nt(a, b):
    return dot(a, b, 1, 1)


def tn(a, b):
    return dot(a, b, 0, 0)


def key_range(packed, i):
    low = max(0, i * BLOCK - BLOCK - BLOCK // 2) if packed else 0
    return low, (i + 1) * BLOCK - low


def head_masks():
    lane = lax.broadcasted_iota(jnp.int32, (1, 2 * HEAD_DIM), 1)
    first = (lane < HEAD_DIM).astype(F32).astype(BF)
    return first, (lane >= HEAD_DIM).astype(F32).astype(BF)


def group_match(rows, tokens):
    row = lax.broadcasted_iota(jnp.int32, (rows, tokens), 0)
    col = lax.broadcasted_iota(jnp.int32, (rows, tokens), 1)
    return (row % (tokens // GROUP)) == (col // GROUP)


def fill_bias(bias_ref, start_ref, packed, i):
    low, count = key_range(packed, i)
    q_pos = i * BLOCK + lax.broadcasted_iota(jnp.int32, (1, BLOCK), 1)
    if packed:
        k_pos = low + lax.broadcasted_iota(jnp.int32, (count, BLOCK), 0)
        allowed = (k_pos <= q_pos) & (k_pos >= start_ref[...])
        bias_ref[0:count, :] = jnp.where(allowed, 0.0, MASKED)
    else:
        k_pos = i * BLOCK + lax.broadcasted_iota(jnp.int32, (BLOCK, BLOCK), 0)
        bias_ref[0:BLOCK, :] = jnp.where(k_pos <= q_pos, 0.0, MASKED)


def add_bias(scores, bias_ref, packed, count):
    if packed:
        return scores + bias_ref[0:count, :]
    last = scores[count - BLOCK :, :] + bias_ref[0:BLOCK, :]
    if count == BLOCK:
        return last
    return jnp.concatenate([scores[: count - BLOCK, :], last], axis=0)


def rms(values):
    return lax.rsqrt(jnp.mean(values * values, axis=-1, keepdims=True) + EPSILON)


def peer(axis, me, d):
    return {axis: me ^ d}


def arrive(partners):
    barrier = pltpu.get_barrier_semaphore()
    for p in partners:
        pl.semaphore_signal(barrier, inc=1, device_id=p, device_id_type=MESH)
    pl.semaphore_wait(barrier, len(partners))


def remote(src, dst, sems, k, where):
    return pltpu.make_async_remote_copy(
        src_ref=src, dst_ref=dst, send_sem=sems[0].at[k], recv_sem=sems[1].at[k],
        device_id=where, device_id_type=MESH,
    )


class Exchange:
    def __init__(self, nb, src, dst, own, sems, base):
        self.nb, self.src, self.dst, self.own, self.sems, self.base = nb, src, dst, own, sems, base
        self.me = lax.axis_index("blk")

    def local(self):
        return pltpu.make_async_copy(
            self.src.at[self.me], self.dst.at[self.me], self.own.at[self.base]
        )

    def copy(self, d):
        return remote(
            self.src.at[self.me ^ d], self.dst.at[self.me], self.sems,
            self.base * (self.nb - 1) + d - 1, peer("blk", self.me, d),
        )

    def start(self):
        self.local().start()
        for d in range(1, self.nb):
            self.copy(d).start()

    def wait(self):
        self.local().wait()
        for d in range(1, self.nb):
            self.copy(d).wait()


def unit(n):
    row = lax.broadcasted_iota(jnp.int32, (n, n), 0)
    col = lax.broadcasted_iota(jnp.int32, (n, n), 1)
    return (row == col).astype(F32).astype(BF)


def split_three(a):
    high = a.astype(BF)
    rest = a - high.astype(F32)
    mid = rest.astype(BF)
    return [high, mid, (rest - mid.astype(F32)).astype(BF)]


def head_rows(heads, width):
    row = lax.broadcasted_iota(jnp.int32, (heads, width), 0)
    col = lax.broadcasted_iota(jnp.int32, (heads, width), 1)
    return (row == col // HEAD_DIM).astype(F32).astype(BF)


def forward_kernel(micros, blocks, nb, x_src, seg_src, cot_src, g1_ref, wq_ref, wk_ref, wv_ref, wo_ref,
                   g2_ref, wc_ref, q_ref, k_ref, v_ref, kt_ref, ob_ref, lse_ref, h_ref, gate_ref,
                   mg_ref, start_ref, x_out, cot_out, x_all, seg_all, bias, o_acc, sums, eye, own,
                   send_sem, recv_sem):
    sems = (send_sem, recv_sem)
    now = pl.program_id(0)
    span = 2 * blocks
    micro, step = now // span, now % span
    width = wo_ref.shape[0]
    pairs = width // (2 * HEAD_DIM)
    me = lax.axis_index("blk")
    xs = [Exchange(nb, x_src.at[m], x_all.at[m], own, sems, m) for m in range(micros)]
    segs = Exchange(nb, seg_src, seg_all, own, sems, micros)
    cots = [
        Exchange(nb, cot_src.at[m], cot_out.at[m], own, sems, micros + 1 + m) for m in range(micros)
    ]
    keep = pltpu.make_async_copy(x_all, x_out, own.at[2 * micros + 1])

    @pl.when(now == 0)
    def _():
        xs[0].local().start()
        eye[...] = unit(width)
        arrive([peer("blk", me, d) for d in range(1, nb)])
        for d in range(1, nb):
            xs[0].copy(d).start()

    @pl.when(step < blocks)
    def _():
        block = me ^ step
        for m in range(micros):
            pl.when((micro == m) & (step == 0))(xs[m].local().wait)
            for d in range(1, nb):
                pl.when((micro == m) & (step == d))(xs[m].copy(d).wait_recv)
        x = x_all[micro, block].astype(F32)
        n1 = (x * rms(x) * g1_ref[...]).astype(BF)
        at = pl.ds(pl.multiple_of(block * BLOCK, BLOCK), BLOCK)
        q_ref[0, at, :] = nn(n1, wq_ref[...]).astype(BF)
        k = nn(n1, wk_ref[...]).astype(BF)
        k_ref[0, at, :] = k
        v_ref[0, at, :] = nn(n1, wv_ref[...]).astype(BF)
        kt_ref[0, :, at] = nt(eye[...], k).astype(BF)

    @pl.when(now == nb - 1)
    def _():
        segs.start()
        for m in range(1, micros):
            xs[m].start()

    @pl.when(now == blocks)
    def _():
        for c in cots:
            c.start()

    @pl.when(now == span)
    def _():
        segs.wait()
        counts = [
            jnp.sum(jnp.sum((seg_all[...] < d).astype(F32), axis=0), keepdims=True)
            for d in range(1, nb * seg_all.shape[1] * seg_all.shape[2] // BLOCK)
        ]
        for b in range(blocks):
            seg = jnp.concatenate([seg_all[b, n : n + 1, :] for n in range(seg_all.shape[1])], axis=1)
            start = jnp.zeros(seg.shape, F32)
            for d, count in enumerate(counts):
                start = jnp.where(seg == d + 1, count, start)
            start_ref[b] = start.astype(jnp.int32)

    masks = head_masks()

    def attend(packed, i):
        low, count = key_range(packed, i)
        fill_bias(bias, start_ref[i], packed, i)
        for hp in range(pairs):
            lanes = slice(hp * 2 * HEAD_DIM, (hp + 1) * 2 * HEAD_DIM)
            q_pair = q_ref[0, i * BLOCK : (i + 1) * BLOCK, lanes]
            k_pair = k_ref[0, low : low + count, lanes]
            v_pair = v_ref[0, low : low + count, lanes]
            o_pair = None
            for h in range(2):
                scores = add_bias(nt(k_pair, q_pair * masks[h]), bias, packed, count)
                top = jnp.max(scores, axis=0, keepdims=True)
                p = jnp.exp((scores - top) * SCALE)
                total = jnp.sum(p, axis=0, keepdims=True)
                o = tn(p.astype(BF), v_pair * masks[h])
                o_pair = o if o_pair is None else o_pair + o
                sums[hp * 2 + h : hp * 2 + h + 1, :] = 1.0 / total
                lse_ref[0, hp * 2 + h : hp * 2 + h + 1, :] = top * SCALE + jnp.log(total)
            o_acc[:, lanes] = o_pair

    for m in range(micros):
        for i in range(blocks):
            pl.when(now == m * span + blocks + i)(functools.partial(attend, m > 0, i))

    @pl.when(step >= blocks)
    def _():
        heads = head_rows(sums.shape[0], width)
        scale = tn(
            jnp.concatenate(split_three(sums[...]), axis=0), jnp.concatenate([heads] * 3, axis=0)
        )
        ob = (o_acc[...] * scale).astype(BF)
        ob_ref[0] = ob
        h = x_all[micro, step - blocks].astype(F32) + nn(ob, wo_ref[...])
        h_ref[0] = h
        n2 = (h * rms(h) * g2_ref[...]).astype(BF)
        logits = nt(wc_ref[...], n2)
        rows = logits.shape[0]
        match = group_match(rows, BLOCK)
        logits = jnp.where(match, logits, MASKED)
        e = jnp.where(match, jnp.exp(logits - jnp.max(logits, axis=1, keepdims=True)), 0.0)
        gate = e / jnp.sum(e, axis=1, keepdims=True)
        gate_ref[...] = gate
        mg = nn(gate.astype(BF), n2).astype(BF).astype(F32)
        half = rows // mg_ref.shape[0]
        for j in range(mg_ref.shape[0]):
            mg_ref[j] = mg[j * half : (j + 1) * half]

    @pl.when(now == span + nb)
    def _():
        keep.start()

    @pl.when(now == micros * span - 1)
    def _():
        keep.wait()
        for x in xs:
            for d in range(1, nb):
                x.copy(d).wait_send()
        for c in cots:
            c.wait()


def gelu_both(u):
    c = 0.7978845608028654
    t = jnp.tanh(c * (u + 0.044715 * (u * u * u)))
    act = 0.5 * u * (1.0 + t)
    slope = 0.5 * (1.0 + t) + 0.5 * u * (1.0 - t * t) * (c * (1.0 + 3 * 0.044715 * (u * u)))
    return act, slope


def same_plane(far, d):
    return {"dp": lax.axis_index("dp") ^ far, "blk": lax.axis_index("blk") ^ d}


def plane_steps(nb):
    return [(far, d) for far in (0, 1) for d in range(0, nb, 2) if far or d]


def experts_kernel(micros, blocks, nb, *refs):
    mg_ref, gate_ref, cot_ref, win_ref, wback_ref = refs[:5]
    eo_ref, dmg_ref, all_ref, factors, gathered, send_sem, recv_sem = refs[5:]
    sems = (send_sem, recv_sem)
    e, c = pl.program_id(0), pl.program_id(1)
    at = e * pl.num_programs(1) + c
    last = pl.num_programs(0) * pl.num_programs(1) - 1
    per = BLOCK // GROUP
    n_exp = factors.shape[0]
    groups = micros * blocks * per
    blk = lax.axis_index("blk")
    kind = blk % n_exp
    steps = [(far, d) for far in (0, 1) for d in range(nb) if far or d]

    def plane_copy(n):
        far, d = steps[n]
        return remote(factors.at[kind ^ (d & 1)], gathered.at[n], sems, n, same_plane(far, d))

    @pl.when(at == 0)
    def _():
        deo = []
        for m in range(micros):
            for i in range(blocks):
                at_rows = (m * blocks + i) * BLOCK
                deo.append(nn(gate_ref[:, at_rows : at_rows + BLOCK].astype(BF), cot_ref[m, i]))
        for j in range(n_exp):
            factors[j, 0] = mg_ref[j].astype(BF)
            factors[j, 1] = jnp.concatenate(
                [d[j * per : (j + 1) * per] for d in deo], axis=0
            ).astype(BF)
        arrive([same_plane(*s) for s in steps])
        for n in range(len(steps)):
            plane_copy(n).start()

    mg, deo = factors[e, 0], factors[e, 1]
    act, slope = gelu_both(nn(mg, win_ref[0]))
    eo_part = nn(act.astype(BF), wback_ref[0])
    du = (slope * nt(deo, wback_ref[0])).astype(BF)
    dmg_part = nt(du, win_ref[0])

    @pl.when(c == 0)
    def _():
        eo_ref[0] = eo_part
        dmg_ref[0] = dmg_part

    @pl.when(c > 0)
    def _():
        eo_ref[0] += eo_part
        dmg_ref[0] += dmg_part

    @pl.when(at == last)
    def _():
        for n in range(len(steps)):
            plane_copy(n).wait()
        for n in range(len(steps) + 1):
            piece = factors[kind] if n == 0 else gathered[n - 1]
            for f in range(2):
                all_ref[f, n * groups : (n + 1) * groups, :] = piece[f]


class Return:
    def __init__(self, nb, buf, out, own, sems, base):
        self.nb, self.buf, self.out, self.own, self.sems, self.base = nb, buf, out, own, sems, base
        self.me = lax.axis_index("blk")

    def local(self):
        return pltpu.make_async_copy(
            self.buf.at[self.me], self.out.at[self.me], self.own.at[self.base]
        )

    def copy(self, d):
        return remote(
            self.buf.at[self.me ^ d], self.out.at[self.me], self.sems,
            self.base * (self.nb - 1) + d - 1, peer("blk", self.me, d),
        )

    def start(self, i, reach=None):
        pl.when(i == self.me)(lambda: self.local().start())
        for d in range(1, reach or self.nb):
            pl.when(i == (self.me ^ d))(lambda d=d: self.copy(d).start())

    def wait(self):
        self.local().wait()
        for d in range(1, self.nb):
            self.copy(d).wait()


class Plan:
    def __init__(self, sems):
        self.sems, self.count, self.sets = sems, 0, {}

    def add(self, name, makers):
        self.sets[name] = list(enumerate(makers, self.count))
        self.count += len(makers)

    def each(self, name):
        for k, maker in self.sets[name]:
            src, dst, where = maker()
            yield remote(src, dst, self.sems, k, where)

    def start(self, name):
        for c in self.each(name):
            c.start()

    def arrived(self, name):
        for c in self.each(name):
            c.wait_recv()

    def sent(self, name):
        for c in self.each(name):
            c.wait_send()


def other_plane(d):
    return {"dp": lax.axis_index("dp") ^ (2 * d)}


def pair_sum(parts):
    while len(parts) > 1:
        parts = [parts[n] + parts[n + 1] for n in range(0, len(parts), 2)]
    return parts[0]


def rows_of(n, size):
    return pl.ds(pl.multiple_of(n * size, size), size)


def backward_kernel(micros, blocks, nb, planes, x_ref, cot_ref, h_ref, gate_ref, eo_ref, dmg_ref, ob_ref,
                    lse_ref, q_ref, k_ref, v_ref, kt_ref, start_ref, g1_ref, g2_ref, wc_ref, wq_ref,
                    wk_ref, wv_ref, wo_ref, factors, win_hbm, wback_hbm, act_ref, gi_ref, flat_ref,
                    small_ref, gin, gback, dh_all, n1_all, dob, delta, dq_all, dk_all, dv_all, dk_acc,
                    dv_acc, gacc, go_acc, bias_own, bias, act_buf, gi_buf, win, wback, ours, theirs, piece, s1,
                    r1, s2, r2, s3, r3, fl, small, few, rs, own, load_sem, ret_send, ret_recv, send_sem,
                    recv_sem):
    now = pl.program_id(0)
    width = wo_ref.shape[0]
    pairs = width // (2 * HEAD_DIM)
    pair_lanes = 2 * HEAD_DIM
    lead, span = micros * blocks, blocks + pairs
    micro = jnp.where(now < lead, now // blocks, (now - lead) // span)
    step = jnp.where(now < lead, now % blocks, (now - lead) % span)
    last = lead + (micros - 1) * span
    blk, dp = lax.axis_index("blk"), lax.axis_index("dp")
    kind, plane = blk % 2, dp // 2
    steps = plane_steps(nb)
    members = len(steps) + 1
    core = lambda: peer("blk", lax.axis_index("blk"), 1)

    def part_of(far, d):
        return ((blk ^ d) // 2) + (nb // 2) * ((dp % 2) ^ far)

    part = part_of(0, 0)
    cut = win.shape[1]
    rets = (ret_send, ret_recv)
    acts = [Return(nb, act_buf.at[m], act_ref.at[m], own, rets, 2 * m) for m in range(micros)]
    gis = [Return(nb, gi_buf.at[m], gi_ref.at[m], own, rets, 2 * m + 1) for m in range(micros)]
    columns = rows_of(part, cut)
    loads = [
        lambda: pltpu.make_async_copy(win_hbm.at[kind, :, columns], win, load_sem.at[0]),
        lambda: pltpu.make_async_copy(wback_hbm.at[kind, columns, :], wback, load_sem.at[1]),
    ]
    rows = width // planes

    def window(which, p, z):
        if which == 0:
            return gin.at[kind, rows_of(z, rows), rows_of(p, cut)]
        at = pl.multiple_of(p * cut + z * rows, rows)
        return gback.at[kind, pl.ds(at, rows), :]

    def slab(which, p):
        if which == 0:
            return gin.at[kind, :, rows_of(p, cut)]
        return gback.at[kind, rows_of(p, cut), :]

    mine = [
        lambda w=w: pltpu.make_async_copy(piece.at[w], window(w, part, plane), load_sem.at[2 + w])
        for w in range(2)
    ]
    y_peer, x_peer = steps[0], steps[1]
    others = range(1, planes)
    both = range(2)
    plan = Plan((send_sem, recv_sem))
    for w in both:
        plan.add(f"rs{w}", [
            lambda d=d, w=w: (ours.at[w, plane ^ d], theirs.at[w, d - 1], other_plane(d)) for d in others
        ])
        plan.add(f"z{w}", [
            lambda d=d, w=w: (piece.at[w], window(w, part, plane), other_plane(d)) for d in others
        ])
        for name, to in ((f"y0{w}", y_peer), (f"x0{w}", x_peer)):
            plan.add(name, [
                lambda w=w, to=to: (piece.at[w], window(w, part, plane), same_plane(*to))
            ])

    def onward(p, z, w, to):
        return window(w, p, z), window(w, p, z), same_plane(*to)

    part_y = part_of(*y_peer)
    for w in both:
        plan.add(f"yx0{w}", [lambda w=w: onward(part_y, plane, w, x_peer)])
        for name, p, to in ((f"y1{w}", part, y_peer), (f"x1{w}", part, x_peer), (f"yx1{w}", part_y, x_peer)):
            plan.add(name, [
                lambda d=d, w=w, p=p, to=to: onward(p, plane ^ d, w, to) for d in others
            ])
        for name, p in zip("oyxd", [part] + [part_of(*t) for t in steps]):
            plan.add(f"c{name}{w}", [lambda w=w, p=p: (slab(w, p), slab(w, p), core())])

    sizes = [width] + [3 * pair_lanes] * pairs
    halves = [n // 2 for n in sizes]
    quarters = [n // 2 // members for n in sizes]

    def held_sum(c):
        return go_acc if c == 0 else gacc.at[c - 1]

    def quarter_at(c, p):
        at = pl.multiple_of(kind * halves[c] + p * quarters[c], quarters[c])
        return pl.ds(at, quarters[c])

    for c in range(pairs + 1):
        n_half, n_quarter = halves[c], quarters[c]
        plan.add(f"ha{c}", [lambda c=c, r=n_half: (s1.at[c, 0:r], r1.at[c, 0:r], core())])
        plan.add(f"hb{c}", [
            lambda c=c, n=n, r=n_quarter: (s2.at[c, n, 0:r], r2.at[c, n, 0:r], same_plane(*steps[n]))
            for n in range(members - 1)
        ])
        plan.add(f"hz{c}", [
            lambda c=c, d=d, r=n_quarter: (s3.at[c, 0:r], r3.at[c, d - 1, 0:r], other_plane(d))
            for d in others
        ])

        def share(c, n):
            ref = fl.at[c, quarter_at(c, part), :]
            return ref, ref, same_plane(*steps[n])

        def side(c):
            ref = fl.at[c, rows_of(kind, halves[c]), :]
            return ref, ref, core()

        plan.add(f"hg{c}", [lambda c=c, n=n: share(c, n) for n in range(members - 1)])
        plan.add(f"hh{c}", [lambda c=c: side(c)])
    near = [(far, d) for far in (0, 1) for d in range(nb) if far or d]
    plan.add("sb", [lambda n=n: (few.at[0], rs.at[n], same_plane(*near[n])) for n in range(len(near))])
    plan.add("sz", [lambda d=d: (few.at[1], rs.at[len(near) + d - 1], other_plane(d)) for d in others])
    assert plan.count <= send_sem.shape[0]

    def chunk_start(c):
        s1[c, 0 : halves[c]] = held_sum(c)[rows_of(1 - kind, halves[c]), :].astype(BF)
        plan.start(f"ha{c}")

    def chunk_b(c):
        plan.arrived(f"ha{c}")
        at = rows_of(kind, halves[c])
        ref = held_sum(c)
        ref[at, :] = ref[at, :] + r1[c, 0 : halves[c]].astype(F32)
        for n, to in enumerate(steps):
            s2[c, n, 0 : quarters[c]] = ref[quarter_at(c, part_of(*to)), :].astype(BF)
        plan.start(f"hb{c}")

    def chunk_z(c):
        plan.arrived(f"hb{c}")
        r = quarters[c]
        total = pair_sum(
            [held_sum(c)[quarter_at(c, part), :]] + [r2[c, n, 0:r].astype(F32) for n in range(members - 1)]
        )
        s3[c, 0:r] = total.astype(BF)
        plan.start(f"hz{c}")

    def chunk_g(c):
        plan.arrived(f"hz{c}")
        r = quarters[c]
        total = pair_sum([s3[c, 0:r].astype(F32)] + [r3[c, d - 1, 0:r].astype(F32) for d in others])
        fl[c, quarter_at(c, part), :] = total.astype(BF)
        plan.start(f"hg{c}")

    def chunk_h(c):
        plan.arrived(f"hg{c}")
        plan.start(f"hh{c}")

    def out_copy(c):
        return pltpu.make_async_copy(fl.at[c], flat_ref.at[c], load_sem.at[4 + c])

    def chunk_done(c):
        plan.arrived(f"hh{c}")
        out_copy(c).start()

    def reduced(w):
        plan.arrived(f"rs{w}")
        total = pair_sum([ours[w, plane].astype(F32)] + [theirs[w, d - 1].astype(F32) for d in others])
        piece[w] = total.astype(BF)
        mine[w]().start()
        for name in ("z", "y0", "x0"):
            plan.start(f"{name}{w}")

    def own_y(w):
        plan.arrived(f"y0{w}")
        plan.start(f"yx0{w}")

    def whole_slice(w):
        mine[w]().wait()
        plan.arrived(f"z{w}")
        for name in ("y1", "x1", "co"):
            plan.start(f"{name}{w}")

    def slice_y(w):
        plan.arrived(f"y1{w}")
        for name in ("yx1", "cy"):
            plan.start(f"{name}{w}")

    def slice_x(w):
        plan.arrived(f"x0{w}")
        plan.arrived(f"x1{w}")
        plan.start(f"cx{w}")

    def slice_d(w):
        plan.arrived(f"yx0{w}")
        plan.arrived(f"yx1{w}")
        plan.start(f"cd{w}")

    stages = [chunk_start, chunk_b, chunk_z, chunk_g, chunk_h, chunk_done]

    @pl.when(now == 0)
    def _():
        for c in loads:
            c().start()
        partners = [peer("blk", blk, d) for d in range(1, nb)]
        partners += [same_plane(1, d) for d in range(nb)] + [other_plane(d) for d in others]
        arrive(partners)
        small[...] = jnp.zeros_like(small)
        go_acc[...] = jnp.zeros_like(go_acc)
        fill_bias(bias_own, None, False, 0)
        for c in loads:
            c().wait()
        mg, deo = factors[0], factors[1]
        act, slope = gelu_both(nn(mg, win[...]))
        du = (slope * nt(deo, wback[...])).astype(BF)
        g_in = tn(mg, du).astype(BF)
        for n in range(planes):
            ours[0, n] = g_in[n * rows : (n + 1) * rows]
        plan.start("rs0")
        g_back = tn(act.astype(BF), deo).astype(BF)
        for n in range(planes):
            ours[1, n] = g_back[n * rows : (n + 1) * rows]
        plan.start("rs1")

    gate_rows = gate_ref.shape[0]

    @pl.when(now < lead)
    def _():
        at = rows_of(step, BLOCK)
        h = h_ref[0]
        cot_b = cot_ref[0, 0]
        dout = cot_b.astype(F32)
        r2_ = rms(h)
        z = h * r2_
        n2 = (z * g2_ref[...]).astype(BF)
        gate = gate_ref[...]
        gate_b = gate.astype(BF)
        gate_low = (gate - gate_b.astype(F32)).astype(BF)
        eo = jnp.concatenate([eo_ref[j] for j in range(eo_ref.shape[0])], axis=0)
        dmg = jnp.concatenate([dmg_ref[j] for j in range(dmg_ref.shape[0])], axis=0).astype(BF)
        eo_b = eo.astype(BF)
        eo_low = (eo - eo_b.astype(F32)).astype(BF)
        mixed = tn(
            jnp.concatenate([gate_b, gate_low, gate_b], axis=0),
            jnp.concatenate([eo_b, eo_b, eo_low], axis=0),
        )
        act_buf[micro, step] = (h + mixed).astype(BF)
        for m in range(micros):
            pl.when(micro == m)(functools.partial(acts[m].start, step))
        dw2 = nt(jnp.concatenate([eo_b, eo_low], axis=0), cot_b)
        dw = dw2[:gate_rows] + dw2[gate_rows:] + nt(dmg, n2)
        wdw = gate * dw
        dlog = (wdw - gate * jnp.sum(wdw, axis=1, keepdims=True)).astype(BF)
        dn2 = tn(
            jnp.concatenate([gate_b, dlog], axis=0),
            jnp.concatenate([dmg, wc_ref[...]], axis=0),
        )
        small[0:gate_rows, :] += nn(dlog, n2)
        small[gate_rows : gate_rows + 1, :] += jnp.sum(dn2 * z, axis=0, keepdims=True)
        a = dn2 * g2_ref[...]
        dh = dout + r2_ * (a - z * jnp.mean(a * z, axis=-1, keepdims=True))
        dh_all[micro, at, :] = dh
        da = dh.astype(BF)
        dob_b = nt(da, wo_ref[...]).astype(BF)
        dob[micro, at, :] = dob_b
        ob = ob_ref[0]
        go_acc[...] += tn(ob, da)
        prod = dob_b.astype(F32) * ob.astype(F32)
        high = prod.astype(BF)
        low = (prod - high.astype(F32)).astype(BF)
        heads = head_rows(delta.shape[1], width)
        delta[micro, :, at] = nt(heads, high) + nt(heads, low)
        x = x_ref[0, step].astype(F32)
        n1_all[micro, at, :] = (x * rms(x) * g1_ref[...]).astype(BF)

    for m in range(1, micros):
        for i in range(blocks):
            pl.when(now == m * blocks + i)(
                functools.partial(fill_bias, bias.at[i], start_ref[i], True, i)
            )

    masks = head_masks()

    def attend(m):
        hp = step
        packed = m > 0
        lanes = rows_of(hp, pair_lanes)
        for i in range(blocks):
            low, count = key_range(packed, i)
            at = slice(i * BLOCK, (i + 1) * BLOCK)
            q_pair, dob_pair = q_ref[0, at, :], dob[m, at, lanes]
            k_pair, v_pair = k_ref[0, low : low + count, :], v_ref[0, low : low + count, :]
            dk_sum = dv_sum = None
            dqs = []
            for h in range(2):
                qm, dm = q_pair * masks[h], dob_pair * masks[h]
                scores = add_bias(nt(k_pair, qm), bias.at[i] if packed else bias_own, packed, count)
                p = jnp.exp(scores * SCALE - lse_ref[0, pl.ds(hp * 2 + h, 1), at])
                dp_ = nt(v_pair, dm)
                ds = (p * (dp_ - delta[m, pl.ds(hp * 2 + h, 1), at])).astype(BF)
                kt = kt_ref[0, h * HEAD_DIM : (h + 1) * HEAD_DIM, low : low + count]
                dqs.append(nn(kt, ds) * SCALE)
                dk_part, dv_part = nn(ds, qm), nn(p.astype(BF), dm)
                dk_sum = dk_part if dk_sum is None else dk_sum + dk_part
                dv_sum = dv_part if dv_sum is None else dv_sum + dv_part
            old = i * BLOCK - low
            dk_acc[at, :] = dk_sum[old:]
            dv_acc[at, :] = dv_sum[old:]
            if old:
                dk_acc[low : i * BLOCK, :] += dk_sum[:old]
                dv_acc[low : i * BLOCK, :] += dv_sum[:old]
            dq_all[at, lanes] = jnp.concatenate(dqs, axis=0).T.astype(BF)
        dk = (dk_acc[...] * SCALE).astype(BF)
        dv = dv_acc[...].astype(BF)
        dk_all[:, lanes] = dk
        dv_all[:, lanes] = dv
        g = tn(jnp.concatenate([dq_all[:, lanes], dk, dv], axis=1), n1_all[m])
        if packed:
            gacc[hp] += g
        else:
            gacc[hp] = g

    for m in range(micros):
        in_phase = (now >= lead) & (micro == m) & (step < pairs)
        pl.when(in_phase)(functools.partial(attend, m))

    in_third = (now >= lead) & (step >= pairs)
    i = blk ^ (nb - 1 - (step - pairs))

    @pl.when(in_third)
    def _():
        at = rows_of(i, BLOCK)
        x = x_ref[0, i].astype(F32)
        r1_ = rms(x)
        z1 = x * r1_
        dn1 = (
            nt(dq_all[at, :], wq_ref[...]) + nt(dk_all[at, :], wk_ref[...]) + nt(dv_all[at, :], wv_ref[...])
        )
        small[gate_rows + 8 : gate_rows + 9, :] += jnp.sum(dn1 * z1, axis=0, keepdims=True)
        b = dn1 * g1_ref[...]
        gi = dh_all[micro, at, :] + r1_ * (b - z1 * jnp.mean(b * z1, axis=-1, keepdims=True))
        gi_buf[micro, i] = gi.astype(BF)

    final = lead + micros * span - 1
    tasks = {}

    def after(at, task, *args):
        tasks.setdefault(min(at, final), []).append(functools.partial(task, *args))

    def far_block(d):
        gis[0].copy(d).start()

    for n, gap in enumerate((0, 2, 5, 8, 10, 12)):
        after(lead - 1 + gap, stages[n], 0)
    for c in range(1, pairs):
        for n, gap in enumerate((0, 1, 3, 5, 6, 7)):
            after(last + c - 1 + gap, stages[n], c)
    c = pairs
    after(last + c - 1, chunk_start, c)
    after(last + c, chunk_b, c)
    after(last + c + 2, chunk_z, c)
    after(blocks, reduced, 0)
    after(lead, reduced, 1)
    after(lead, own_y, 0)
    after(lead + 2, whole_slice, 0)
    after(lead + 2, own_y, 1)
    after(last - 1, slice_y, 0)
    after(last - 1, whole_slice, 1)
    after(last + pairs - 2, slice_y, 1)
    after(last + pairs - 2, slice_x, 0)
    after(final, slice_x, 1)
    after(final, slice_d, 0)
    for d in range(2, nb):
        after(last + 2 * (d - 2), far_block, d)
    for at, todo in tasks.items():
        if at < final:

            @pl.when(now == at)
            def _(todo=todo):
                for task in todo:
                    task()

    @pl.when(in_third)
    def _():
        for m in range(micros):
            pl.when(micro == m)(functools.partial(gis[m].start, i, 2 if m == 0 else nb))

    @pl.when(now == final)
    def _():
        per = gate_rows // 2
        few[0] = jnp.concatenate(
            [jnp.sum(small[n * per : (n + 1) * per, :], axis=0, keepdims=True) for n in range(2)]
            + [small[gate_rows : gate_rows + 1, :], small[gate_rows + 8 : gate_rows + 9, :]]
            + [jnp.zeros((4, width), F32)],
            axis=0,
        )
        plan.start("sb")
        for task in tasks[final]:
            task()
        chunk_g(c)
        plan.arrived("sb")
        few[1] = pair_sum([few[0]] + [rs[n] for n in range(len(near))])
        plan.start("sz")
        chunk_h(c)
        slice_d(1)
        chunk_done(c)
        plan.arrived("sz")
        small_ref[...] = pair_sum([few[1]] + [rs[len(near) + d - 1] for d in others])
        for w in both:
            for name in "oyxd":
                plan.arrived(f"c{name}{w}")
        for n in range(pairs + 1):
            out_copy(n).wait()
        for name in plan.sets:
            plan.sent(name)
        for r in acts + gis:
            r.wait()


def whole(shape):
    return pl.BlockSpec(shape, lambda *_: (0,) * len(shape))


def held(shape):
    return pl.BlockSpec(shape, lambda *_: (0,) * len(shape), pipeline_mode=pl.Buffered(1))


ANY = pl.BlockSpec(memory_space=pl.ANY)
DMA = pltpu.SemaphoreType.DMA


def shaped(shape, dtype):
    return jax.ShapeDtypeStruct(shape, dtype)


def params(number):
    return pltpu.CompilerParams(
        vmem_limit_bytes=VMEM_LIMIT, collective_id=number, has_side_effects=True
    )


def forward_call(x, seg, cot, g1, wq, wk, wv, wo, g2, wc):
    nb = lax.axis_size("blk")
    micros, _, rows_in, width = x.shape
    length = nb * rows_in
    blocks = length // BLOCK
    assert x.shape[1] == nb and rows_in == BLOCK
    rows = wc.shape[0]
    heads = width // HEAD_DIM
    per = BLOCK // GROUP
    experts = rows // per
    span = 2 * blocks
    phase = lambda s: jnp.maximum(s % span - blocks, 0)
    whole_micro = lambda a, b: pl.BlockSpec((1, a, b), lambda s: (s // span, 0, 0))
    flat = lambda s: (s // span) * blocks + phase(s)
    moves = 2 * micros + 1
    return pl.pallas_call(
        functools.partial(forward_kernel, micros, blocks, nb),
        grid=(micros * span,),
        in_specs=[ANY, ANY, ANY] + [held(a.shape) for a in (g1, wq, wk, wv, wo, g2, wc)],
        out_specs=[
            whole_micro(length, width), whole_micro(length, width), whole_micro(length, width),
            whole_micro(width, length),
            pl.BlockSpec((1, BLOCK, width), lambda s: (s // span, phase(s), 0)),
            pl.BlockSpec((1, heads, BLOCK), lambda s: (s // span, 0, phase(s))),
            pl.BlockSpec((1, BLOCK, width), lambda s: (s // span, phase(s), 0)),
            pl.BlockSpec((rows, BLOCK), lambda s: (0, flat(s))),
            pl.BlockSpec((experts, per, width), lambda s: (0, flat(s), 0)),
            whole((blocks, 1, BLOCK)), ANY, ANY,
        ],
        out_shape=[
            shaped((micros, length, width), BF), shaped((micros, length, width), BF),
            shaped((micros, length, width), BF), shaped((micros, width, length), BF),
            shaped((micros, length, width), BF), shaped((micros, heads, length), F32),
            shaped((micros, length, width), F32), shaped((rows, micros * length), F32),
            shaped((experts, micros * length // GROUP, width), F32),
            shaped((blocks, 1, BLOCK), jnp.int32), shaped(x.shape, BF), shaped(x.shape, BF),
        ],
        scratch_shapes=[
            pltpu.VMEM(x.shape, BF), pltpu.VMEM(seg.shape, seg.dtype),
            pltpu.VMEM((length, BLOCK), F32), pltpu.VMEM((BLOCK, width), F32),
            pltpu.VMEM((heads, BLOCK), F32), pltpu.VMEM((width, width), BF),
            DMA((moves + 1,)), DMA((moves * (nb - 1),)), DMA((moves * (nb - 1),)),
        ],
        compiler_params=params(1),
        name="attention_forward",
    )(x, seg, cot, g1, wq, wk, wv, wo, g2, wc)


def experts_call(mg, gate, cot, w_in, w_back):
    micros, nb, _, width = cot.shape
    experts, groups, _ = mg.shape
    ff = w_in.shape[2]
    blocks = gate.shape[1] // BLOCK // micros
    chunk = min(CHUNK, ff)
    by_expert = lambda n: pl.BlockSpec((1, n, width), lambda e, c: (e, 0, 0))
    members = 2 * nb
    return pl.pallas_call(
        functools.partial(experts_kernel, micros, blocks, nb),
        grid=(experts, ff // chunk),
        in_specs=[
            held(mg.shape), held(gate.shape), held(cot.shape),
            pl.BlockSpec((1, width, chunk), lambda e, c: (e, 0, c)),
            pl.BlockSpec((1, chunk, width), lambda e, c: (e, c, 0)),
        ],
        out_specs=[by_expert(groups)] * 2 + [whole((2, members * groups, width))],
        out_shape=[shaped((experts, groups, width), F32)] * 2
        + [shaped((2, members * groups, width), BF)],
        scratch_shapes=[
            pltpu.VMEM((experts, 2, groups, width), BF),
            pltpu.VMEM((members - 1, 2, groups, width), BF), DMA((members - 1,)), DMA((members - 1,)),
        ],
        compiler_params=params(2),
        name="experts",
    )(mg, gate, cot, w_in, w_back)


def backward_call(x, cot, h, gate, eo, dmg, ob, lse, q, k, v, kt, start, g1, g2, wc, wq, wk, wv, wo,
                  factors, w_in, w_back):
    micros, nb, _, width = x.shape
    planes = lax.axis_size("dp") // 2
    length = q.shape[1]
    blocks = length // BLOCK
    rows = wc.shape[0]
    per = BLOCK // GROUP
    experts = rows // per
    heads = width // HEAD_DIM
    pairs = heads // 2
    ff = w_in.shape[2]
    cut = ff // nb
    assert cut == width
    members = len(plane_steps(nb)) + 1
    lead, span = micros * blocks, blocks + pairs
    flat = lambda s: jnp.minimum(s, lead - 1)
    m_late = lambda s: jnp.maximum(s - lead, 0) // span
    m_of = lambda s: jnp.where(s < lead, s // blocks, m_late(s))
    pair_of = lambda s: jnp.minimum(jnp.maximum(s - lead, 0) % span, pairs - 1)
    row_block = pl.BlockSpec((1, BLOCK, width), lambda s: (flat(s) // blocks, flat(s) % blocks, 0))
    group_block = pl.BlockSpec((experts, per, width), lambda s: (0, flat(s), 0))
    pair_block = pl.BlockSpec((1, length, 2 * HEAD_DIM), lambda s: (m_late(s), 0, pair_of(s)))
    piece = (2, width // planes, cut)
    chunk = width
    chunks = pairs + 1
    half = chunk // 2
    quarter = half // members
    reach = max(key_range(True, i)[1] for i in range(blocks))
    small = (rows + 16, width)
    few = (8, width)
    vm = pltpu.VMEM
    copies = 96 + 16 * chunks + 32 * planes
    return pl.pallas_call(
        functools.partial(backward_kernel, micros, blocks, nb, planes),
        grid=(lead + micros * span,),
        in_specs=[
            pl.BlockSpec((1, nb, BLOCK, width), lambda s: (m_of(s), 0, 0, 0)),
            pl.BlockSpec((1, 1, BLOCK, width), lambda s: (flat(s) // blocks, flat(s) % blocks, 0, 0)),
            row_block,
            pl.BlockSpec((rows, BLOCK), lambda s: (0, flat(s))),
            group_block, group_block, row_block,
            pl.BlockSpec((1, heads, length), lambda s: (m_late(s), 0, 0)),
            pair_block, pair_block, pair_block,
            pl.BlockSpec((1, 2 * HEAD_DIM, length), lambda s: (m_late(s), pair_of(s), 0)),
        ] + [held(a.shape) for a in (start, g1, g2, wc, wq, wk, wv, wo, factors)] + [ANY, ANY],
        out_specs=[ANY, ANY, ANY, whole(few), ANY, ANY],
        out_shape=[
            shaped(x.shape, BF), shaped(x.shape, BF), shaped((chunks, chunk, width), BF),
            shaped(few, F32), shaped(w_in.shape, BF), shaped(w_back.shape, BF),
        ],
        scratch_shapes=[
            vm((micros, length, width), F32), vm((micros, length, width), BF),
            vm((micros, length, width), BF), vm((micros, heads, length), F32), vm((length, width), BF), vm((length, width), BF),
            vm((length, width), BF), vm((length, 2 * HEAD_DIM), F32), vm((length, 2 * HEAD_DIM), F32),
            vm((pairs, 6 * HEAD_DIM, width), F32), vm((width, width), F32), vm((BLOCK, BLOCK), F32),
            vm((blocks, reach, BLOCK), F32),
            vm(x.shape, BF), vm(x.shape, BF), vm((width, cut), BF), vm((cut, width), BF),
            vm((2, planes) + piece[1:], BF), vm((2, planes - 1) + piece[1:], BF), vm(piece, BF),
            vm((chunks, half, width), BF), vm((chunks, half, width), BF),
            vm((chunks, members - 1, quarter, width), BF), vm((chunks, members - 1, quarter, width), BF),
            vm((chunks, quarter, width), BF), vm((chunks, planes - 1, quarter, width), BF),
            vm((chunks, chunk, width), BF), vm(small, F32), vm((2,) + few, F32),
            vm((2 * nb + planes - 2,) + few, F32),
            DMA((2 * micros,)), DMA((5 + pairs,)), DMA((2 * micros * (nb - 1),)),
            DMA((2 * micros * (nb - 1),)), DMA((copies,)), DMA((copies,)),
        ],
        compiler_params=params(3),
        name="attention_backward",
    )(x, cot, h, gate, eo, dmg, ob, lse, q, k, v, kt, start, g1, g2, wc, wq, wk, wv, wo, factors, w_in,
      w_back)


def local(block_input, segment_ids, gain_one, w_query, w_key, w_value, w_out, gain_two, w_ctrl,
          w_in, w_back, cotangent):
    micros, seqs, rows, width = block_input.shape
    experts, _, ff = w_in.shape
    nb = lax.axis_size("blk")
    per = BLOCK // GROUP
    g1, g2 = gain_one.reshape(1, width), gain_two.reshape(1, width)
    wc = jnp.repeat(w_ctrl.T, per, axis=0)
    seg = segment_ids.reshape(nb, 2, rows // 2)
    q, k, v, kt, ob, lse, h, gate, mg, start, x, cot = forward_call(
        block_input, seg, cotangent, g1, w_query, w_key, w_value, w_out, g2, wc
    )
    eo, dmg, factors = experts_call(mg, gate, cot, w_in, w_back)
    acts, gis, flat, small, grad_in, grad_back = backward_call(
        x, cot, h, gate, eo, dmg, ob, lse, q, k, v, kt, start, g1, g2, wc, w_query, w_key, w_value,
        w_out, factors, w_in, w_back,
    )
    lanes = 2 * HEAD_DIM
    one = lambda n: flat[1:, n * lanes : (n + 1) * lanes].reshape(width, width).astype(F32).T
    return (
        acts, gis, small[3], one(0), one(1), one(2), flat[0].astype(F32), small[2], small[:experts].T,
        grad_in.astype(F32), grad_back.astype(F32),
    )


def solution(mesh):
    data = P(None, "dp", "blk", None)
    in_specs = (data, P("dp", "blk")) + (P(),) * 9 + (data,)
    out_specs = (data, data) + (P(),) * 9
    return jax.shard_map(local, mesh=mesh, in_specs=in_specs, out_specs=out_specs, check_vma=False)
```

profile of v0, /device:TPU:0, one launch (start us, length us, event | category | flops | bytes accessed | tf_op | source)
XLA Modules:
  0.0 246.5 jit_solution(18162998562423976548)
XLA Ops:
  0.6 0.0 copy-start
  0.7 0.7 copy-done
  1.3 1.3 reshape.45.seg_src
  2.6 0.6 broadcast_bitcast_fusion.wc_ref
  3.2 70.4 %attention_forward.1 = (bf16[2,1024,512]{2,1,0:T(8,128)(2,1)}, bf16[2,1024,512]{2,1,0:T(8,128)(2,1)}, bf16[2,1024,512]{2,1,0:T(8,128)(2,1)}, bf16[2,512,1024]{2,...) custom-call(bf16[2,4,256,512]{3,2,1,0:T(8,128)(2,1)} %x_src.1, ...), custom_call_target="tpu_custom_call" | custom-call | tf_op jit(solution)/shard_map/attention_forward/pallas_call | solution.py:867
  73.6 18.5 %experts.1 = (f32[2,64,512]{2,1,0:T(8,128)}, f32[2,64,512]{2,1,0:T(8,128)}, bf16[2,512,512]{2,1,0:T(8,128)(2,1)}) custom-call(f32[2,64,512]{2,1,0:T(8,128)} %get-tuple-element.36.refs_0_, f32[16,2048]{1,0:T(8,128)} %get-tuple-element.35.refs_1_.gate_ref, bf16[2,4,256,512]{3,2,1,0:T(8,128)(2,1)} %get-tuple-element.33.refs_2_.cot_ref, ...), custom_call_target="tpu_custom_call" | custom-call | tf_op jit(solution)/shard_map/experts/pallas_call | solution.py:908
  92.1 128.3 %attention_backward.1 = (bf16[2,4,256,512]{3,2,1,0:T(8,128)(2,1)}, bf16[2,4,256,512]{3,2,1,0:T(8,128)(2,1)}, bf16[5,512,512]{2,1,0:T(8,128)(2,1)}, f32[8,512]{1,...) custom-call(bf16[2,4,256,512]{3,2,1,0:T(8,128)(2,1)} %get-tuple-element.32.x_ref, ...), custom_call_target="tpu_custom_call" | custom-call | tf_op jit(solution)/shard_map/attention_backward/pallas_call | solution.py:961
  220.4 1.3 slice_bitcast_fusion
  221.7 1.4 fusion.1
  223.1 2.1 bitcast_convert_fusion
  225.2 1.5 fusion
  226.7 0.2 bitcast_convert_fusion.3
  226.9 1.3 copy.23
  228.2 0.3 bitcast_convert_fusion.1
  228.5 1.3 copy.25
  229.9 1.3 copy.24
  231.2 0.0 copy-start.2
  231.2 6.8 %convert_element_type.29 = f32[2,512,2048]{2,1,0:T(8,128)} convert(bf16[2,512,2048]{2,1,0:T(8,128)(2,1)} %get-tuple-element.51) | non-fusion elementwise | flops 2097152 | bytes 12582912 | tf_op jit(solution)/shard_map/convert_element_type | solution.py:1022
  238.0 0.0 copy-done.2
  238.0 0.0 copy-start.4
  238.0 4.6 %convert_element_type.30 = f32[2,2048,512]{2,1,0:T(8,128)} convert(bf16[2,2048,512]{2,1,0:T(8,128)(2,1)S(1)} %copy-done.2) | non-fusion elementwise | flops 2097152 | bytes 12582912 | tf_op jit(solution)/shard_map/convert_element_type | solution.py:1022
  242.6 0.0 copy-done.4
  242.6 0.0 copy-start.3
  242.6 0.0 copy-start.1
  242.6 1.3 copy.28
  243.9 1.0 copy-done.3
  244.9 1.3 copy.29
  246.2 0.0 copy-done.1
Async XLA Ops:
  0.6 0.7 copy-start
  231.2 6.8 %copy-start.2 = (bf16[2,2048,512]{2,1,0:T(8,128)(2,1)S(1)}, bf16[2,2048,512]{2,1,0:T(8,128)(2,1)}, u32[]{:S(2)}) copy-start(bf16[2,2048,512]{2,1,0:T(8,128)(2,1)} %get-tuple-element.52) | copy-start | bytes 12582916
  238.0 4.6 %copy-start.4 = (bf16[2,4,256,512]{3,2,1,0:T(8,128)(2,1)S(1)}, bf16[2,4,256,512]{3,2,1,0:T(8,128)(2,1)}, u32[]{:S(2)}) copy-start(bf16[2,4,256,512]{3,2,1,0:T(8,128)(2,1)} %get-tuple-element.71) | copy-start | bytes 6291460
  242.6 2.3 copy-start.3
  242.6 3.7 %copy-start.1 = (bf16[512,2]{0,1:T(2,128)(2,1)S(1)}, bf16[512,2]{0,1:T(2,128)(2,1)}, u32[]{:S(2)}) copy-start(bf16[512,2]{0,1:T(2,128)(2,1)} %param.20) | copy-start | bytes 6148
where the time goes:
time: 247 us
  Pallas kernels  217 us (88%)
  local copies, waits for them, and re-layouts  14.4 us (6%)
  other arithmetic  14.1 us (6%)
    pallas_call x1, Pallas kernels, backward_call(): pl.pallas_call(functools.partial(backward_kernel, micros, blocks, nb, pla...  128 us
    pallas_call x1, Pallas kernels, forward_call(): pl.pallas_call(functools.partial(forward_kernel, micros, blocks, nb), gri...  70.4 us
    pallas_call x1, Pallas kernels, experts_call(): pl.pallas_call(functools.partial(experts_kernel, micros, blocks, nb), gri...  18.5 us
    convert_element_type x1, other arithmetic, local(): grad_in.astype(F32)  6.8 us

commit v1 on v0

--- a/solution.py
+++ b/solution.py
@@ -495,35 +495,34 @@
         for name, p in zip("oyxd", [part] + [part_of(*t) for t in steps]):
             plan.add(f"c{name}{w}", [lambda w=w, p=p: (slab(w, p), slab(w, p), core())])
 
-    sizes = [width] + [3 * pair_lanes] * pairs
-    halves = [n // 2 for n in sizes]
-    quarters = [n // 2 // members for n in sizes]
+    wides = [width] + [3 * pair_lanes] * pairs
+    half, quarter = width // 2, width // 2 // members
 
     def held_sum(c):
         return go_acc if c == 0 else gacc.at[c - 1]
 
-    def quarter_at(c, p):
-        at = pl.multiple_of(kind * halves[c] + p * quarters[c], quarters[c])
-        return pl.ds(at, quarters[c])
+    def quarter_at(p):
+        at = pl.multiple_of(kind * half + p * quarter, quarter)
+        return pl.ds(at, quarter)
 
     for c in range(pairs + 1):
-        n_half, n_quarter = halves[c], quarters[c]
-        plan.add(f"ha{c}", [lambda c=c, r=n_half: (s1.at[c, 0:r], r1.at[c, 0:r], core())])
+        wide = wides[c]
+        plan.add(f"ha{c}", [lambda c=c, w=wide: (s1.at[c, :, 0:w], r1.at[c, :, 0:w], core())])
         plan.add(f"hb{c}", [
-            lambda c=c, n=n, r=n_quarter: (s2.at[c, n, 0:r], r2.at[c, n, 0:r], same_plane(*steps[n]))
+            lambda c=c, n=n, w=wide: (s2.at[c, n, :, 0:w], r2.at[c, n, :, 0:w], same_plane(*steps[n]))
             for n in range(members - 1)
         ])
         plan.add(f"hz{c}", [
-            lambda c=c, d=d, r=n_quarter: (s3.at[c, 0:r], r3.at[c, d - 1, 0:r], other_plane(d))
+            lambda c=c, d=d, w=wide: (s3.at[c, :, 0:w], r3.at[c, d - 1, :, 0:w], other_plane(d))
             for d in others
         ])
 
         def share(c, n):
-            ref = fl.at[c, quarter_at(c, part), :]
+            ref = fl.at[c, quarter_at(part), 0 : wides[c]]
             return ref, ref, same_plane(*steps[n])
 
         def side(c):
-            ref = fl.at[c, rows_of(kind, halves[c]), :]
+            ref = fl.at[c, rows_of(kind, half), 0 : wides[c]]
             return ref, ref, core()
 
         plan.add(f"hg{c}", [lambda c=c, n=n: share(c, n) for n in range(members - 1)])
@@ -534,32 +533,32 @@
     assert plan.count <= send_sem.shape[0]
 
     def chunk_start(c):
-        s1[c, 0 : halves[c]] = held_sum(c)[rows_of(1 - kind, halves[c]), :].astype(BF)
+        s1[c, :, 0 : wides[c]] = held_sum(c)[rows_of(1 - kind, half), :].astype(BF)
         plan.start(f"ha{c}")
 
     def chunk_b(c):
         plan.arrived(f"ha{c}")
-        at = rows_of(kind, halves[c])
+        at = rows_of(kind, half)
         ref = held_sum(c)
-        ref[at, :] = ref[at, :] + r1[c, 0 : halves[c]].astype(F32)
+        ref[at, :] = ref[at, :] + r1[c, :, 0 : wides[c]].astype(F32)
         for n, to in enumerate(steps):
-            s2[c, n, 0 : quarters[c]] = ref[quarter_at(c, part_of(*to)), :].astype(BF)
+            s2[c, n, :, 0 : wides[c]] = ref[quarter_at(part_of(*to)), :].astype(BF)
         plan.start(f"hb{c}")
 
     def chunk_z(c):
         plan.arrived(f"hb{c}")
-        r = quarters[c]
+        w = wides[c]
         total = pair_sum(
-            [held_sum(c)[quarter_at(c, part), :]] + [r2[c, n, 0:r].astype(F32) for n in range(members - 1)]
+            [held_sum(c)[quarter_at(part), :]] + [r2[c, n, :, 0:w].astype(F32) for n in range(members - 1)]
         )
-        s3[c, 0:r] = total.astype(BF)
+        s3[c, :, 0:w] = total.astype(BF)
         plan.start(f"hz{c}")
 
     def chunk_g(c):
         plan.arrived(f"hz{c}")
-        r = quarters[c]
-        total = pair_sum([s3[c, 0:r].astype(F32)] + [r3[c, d - 1, 0:r].astype(F32) for d in others])
-        fl[c, quarter_at(c, part), :] = total.astype(BF)
+        w = wides[c]
+        total = pair_sum([s3[c, :, 0:w].astype(F32)] + [r3[c, d - 1, :, 0:w].astype(F32) for d in others])
+        fl[c, quarter_at(part), 0:w] = total.astype(BF)
         plan.start(f"hg{c}")
 
     def chunk_h(c):
@@ -724,7 +723,7 @@
         dv = dv_acc[...].astype(BF)
         dk_all[:, lanes] = dk
         dv_all[:, lanes] = dv
-        g = tn(jnp.concatenate([dq_all[:, lanes], dk, dv], axis=1), n1_all[m])
+        g = tn(n1_all[m], jnp.concatenate([dq_all[:, lanes], dk, dv], axis=1))
         if packed:
             gacc[hp] += g
         else:
@@ -980,7 +979,7 @@
             vm((micros, length, width), F32), vm((micros, length, width), BF),
             vm((micros, length, width), BF), vm((micros, heads, length), F32), vm((length, width), BF), vm((length, width), BF),
             vm((length, width), BF), vm((length, 2 * HEAD_DIM), F32), vm((length, 2 * HEAD_DIM), F32),
-            vm((pairs, 6 * HEAD_DIM, width), F32), vm((width, width), F32), vm((BLOCK, BLOCK), F32),
+            vm((pairs, width, 6 * HEAD_DIM), F32), vm((width, width), F32), vm((BLOCK, BLOCK), F32),
             vm((blocks, reach, BLOCK), F32),
             vm(x.shape, BF), vm(x.shape, BF), vm((width, cut), BF), vm((cut, width), BF),
             vm((2, planes) + piece[1:], BF), vm((2, planes - 1) + piece[1:], BF), vm(piece, BF),
@@ -1016,7 +1015,9 @@
         w_out, factors, w_in, w_back,
     )
     lanes = 2 * HEAD_DIM
-    one = lambda n: flat[1:, n * lanes : (n + 1) * lanes].reshape(width, width).astype(F32).T
+    one = lambda n: jnp.concatenate(
+        [flat[c, :, n * lanes : (n + 1) * lanes] for c in range(1, flat.shape[0])], axis=1
+    ).astype(F32)
     return (
         acts, gis, small[3], one(0), one(1), one(2), flat[0].astype(F32), small[2], small[:experts].T,
         grad_in.astype(F32), grad_back.astype(F32),

time: 247 us -> 244 us (0.988)
  local copies, waits for them, and re-layouts: 14.4 us -> 11.4 us
    transpose x3 -> x0, local copies, waits for them, and re-layouts: 3.93 us -> none  [local(): flat[1:, n * lanes:(n + 1) * lanes].reshape(width, width).astype(F32)]
    convert_element_type x0 -> x2, other arithmetic: none -> 2.49 us  [local(): one = lambda n: jnp.concatenate([flat[c, :, n * lanes:(n + 1) * lanes] fo...]
    unnamed x12 -> x14, local copies, waits for them, and re-layouts: 4.36 us -> 5.18 us
where the time goes in v1:
time: 244 us; the launch traced here: 243 us
  Pallas kernels  217 us (89%)
  other arithmetic  13.7 us (6%)
  local copies, waits for them, and re-layouts  11.4 us (5%)
    pallas_call x1, Pallas kernels, backward_call(): pl.pallas_call(functools.partial(backward_kernel, micros, blocks, nb, pla...  128 us
    pallas_call x1, Pallas kernels, forward_call(): pl.pallas_call(functools.partial(forward_kernel, micros, blocks, nb), gri...  70.6 us
    pallas_call x1, Pallas kernels, experts_call(): pl.pallas_call(functools.partial(experts_kernel, micros, blocks, nb), gri...  18.5 us
    unnamed x14, local copies, waits for them, and re-layouts  5.18 us

profile of v1, /device:TPU:0, one launch (start us, length us, event | category | flops | bytes accessed | tf_op | source)
XLA Modules:
  0.0 243.5 jit_solution(14895396564749805758)
XLA Ops:
  0.6 0.0 copy-start
  0.7 0.7 copy-done
  1.3 1.3 reshape.36.seg_src
  2.6 0.6 broadcast_bitcast_fusion.wc_ref
  3.2 70.6 %attention_forward.1 = (bf16[2,1024,512]{2,1,0:T(8,128)(2,1)}, bf16[2,1024,512]{2,1,0:T(8,128)(2,1)}, bf16[2,1024,512]{2,1,0:T(8,128)(2,1)}, bf16[2,512,1024]{2,...) custom-call(bf16[2,4,256,512]{3,2,1,0:T(8,128)(2,1)} %x_src.1, ...), custom_call_target="tpu_custom_call" | custom-call | tf_op jit(solution)/shard_map/attention_forward/pallas_call | solution.py:866
  73.9 18.5 %experts.1 = (f32[2,64,512]{2,1,0:T(8,128)}, f32[2,64,512]{2,1,0:T(8,128)}, bf16[2,512,512]{2,1,0:T(8,128)(2,1)}) custom-call(f32[2,64,512]{2,1,0:T(8,128)} %get-tuple-element.36.refs_0_, f32[16,2048]{1,0:T(8,128)} %get-tuple-element.35.refs_1_.gate_ref, bf16[2,4,256,512]{3,2,1,0:T(8,128)(2,1)} %get-tuple-element.33.refs_2_.cot_ref, ...), custom_call_target="tpu_custom_call" | custom-call | tf_op jit(solution)/shard_map/experts/pallas_call | solution.py:907
  92.3 128.4 %attention_backward.1 = (bf16[2,4,256,512]{3,2,1,0:T(8,128)(2,1)}, bf16[2,4,256,512]{3,2,1,0:T(8,128)(2,1)}, bf16[5,512,512]{2,1,0:T(8,128)(2,1)}, f32[8,512]{1,...) custom-call(bf16[2,4,256,512]{3,2,1,0:T(8,128)(2,1)} %get-tuple-element.32.x_ref, ...), custom_call_target="tpu_custom_call" | custom-call | tf_op jit(solution)/shard_map/attention_backward/pallas_call | solution.py:960
  220.7 1.3 slice_bitcast_fusion.12
  222.0 1.4 fusion
  223.4 2.1 bitcast_convert_fusion
  225.5 1.6 slice_bitcast_fusion.3
  227.1 0.0 copy-start.3
  227.1 1.0 maximum_convert_fusion.2
  228.2 1.4 maximum_convert_fusion
  229.6 0.8 copy-done.3
  230.5 0.0 copy-start.2
  230.5 4.4 %convert_element_type.26 = f32[2,512,2048]{2,1,0:T(8,128)} convert(bf16[2,512,2048]{2,1,0:T(8,128)(2,1)S(1)} %copy-done.3) | non-fusion elementwise | flops 2097152 | bytes 12582912 | tf_op jit(solution)/shard_map/convert_element_type | solution.py:1023
  234.9 0.0 copy-done.2
  234.9 0.0 copy-start.5
  234.9 4.6 %convert_element_type.27 = f32[2,2048,512]{2,1,0:T(8,128)} convert(bf16[2,2048,512]{2,1,0:T(8,128)(2,1)S(1)} %copy-done.2) | non-fusion elementwise | flops 2097152 | bytes 12582912 | tf_op jit(solution)/shard_map/convert_element_type | solution.py:1023
  239.5 0.0 copy-done.5
  239.5 0.0 copy-start.4
  239.5 0.0 copy-start.1
  239.5 1.3 copy.25
  240.8 1.0 copy-done.4
  241.9 1.3 copy.26
  243.2 0.0 copy-done.1
Async XLA Ops:
  0.6 0.7 copy-start
  227.1 3.3 %copy-start.3 = (bf16[2,512,2048]{2,1,0:T(8,128)(2,1)S(1)}, bf16[2,512,2048]{2,1,0:T(8,128)(2,1)}, u32[]{:S(2)}) copy-start(bf16[2,512,2048]{2,1,0:T(8,128)(2,1)} %get-tuple-element.51) | copy-start | bytes 12582916
  230.5 4.5 %copy-start.2 = (bf16[2,2048,512]{2,1,0:T(8,128)(2,1)S(1)}, bf16[2,2048,512]{2,1,0:T(8,128)(2,1)}, u32[]{:S(2)}) copy-start(bf16[2,2048,512]{2,1,0:T(8,128)(2,1)} %get-tuple-element.52) | copy-start | bytes 12582916
  234.9 4.6 %copy-start.5 = (bf16[2,4,256,512]{3,2,1,0:T(8,128)(2,1)S(1)}, bf16[2,4,256,512]{3,2,1,0:T(8,128)(2,1)}, u32[]{:S(2)}) copy-start(bf16[2,4,256,512]{3,2,1,0:T(8,128)(2,1)} %get-tuple-element.80) | copy-start | bytes 6291460
  239.5 2.3 copy-start.4
  239.5 3.7 %copy-start.1 = (bf16[512,2]{0,1:T(2,128)(2,1)S(1)}, bf16[512,2]{0,1:T(2,128)(2,1)}, u32[]{:S(2)}) copy-start(bf16[512,2]{0,1:T(2,128)(2,1)} %param.20) | copy-start | bytes 6148
